TPU v7x, 32 devices: a whole 2x2x4 slice. The times are simulated.
32 devices in a mesh: seq: 8 (over y, x, core), batch: 4 (over z).
Axes of the slice: x: 2, y: 2, z: 4, core: 2. Of those that a mesh axis runs over, the one named last changes fastest.
Arguments:
- inputs: bfloat16 [4, 1024, 1024], P('batch', 'seq'), may hold values from -6 to 6
- teacher: bfloat16 [4, 1024, 1024], P('batch', 'seq'), may hold values from -6 to 6
- lengths: int32 [4], P('batch'), may hold values from 960 to 1023
- variate_ids: int32 [4, 1024], P('batch', 'seq'), may hold values from 0 to 15, as said below
- time_ids: int32 [4, 1024], P('batch', 'seq'), may hold values from 0 to 1008, as said below
- observed: int32 [4, 1024], P('batch', 'seq'), may hold values from 0 to 1, as said below
- attend_weight: float32 [3, 1024, 1024], P(None, ('seq', 'batch')), may hold values from -0.1875 to 0.1875
- output_weight: float32 [1024, 1024], P(('seq', 'batch')), may hold values from -5 to 5
- expand_weight: float32 [2, 1024, 4096], P(None, ('seq', 'batch')), may hold values from -0.1875 to 0.1875
- reduce_weight: float32 [4096, 1024], P(('seq', 'batch')), may hold values from -0.09375 to 0.09375
- norm_gains: float32 [2, 1024], replicated, may hold values from 0.25 to 2.8
- variate_bias: float32 [2, 16], replicated, may hold values from -4 to 4
- attend_first: float32 [3, 1024, 1024], P(None, ('seq', 'batch')), may hold values from -0.00015258789 to 0.00015258789
- output_first: float32 [1024, 1024], P(('seq', 'batch')), may hold values from -0.00015258789 to 0.00015258789
- expand_first: float32 [2, 1024, 4096], P(None, ('seq', 'batch')), may hold values from -0.00015258789 to 0.00015258789
- reduce_first: float32 [4096, 1024], P(('seq', 'batch')), may hold values from -0.00015258789 to 0.00015258789
- gains_first: float32 [2, 1024], replicated, may hold values from -0.00048828125 to 0.00048828125
- bias_first: float32 [2, 16], replicated, may hold values from -0.0017089844 to 0.0017089844
- attend_second: float32 [3, 1024, 1024], P(None, ('seq', 'batch')), may hold values from 1.2159348e-09 to 4.863739e-09
- output_second: float32 [1024, 1024], P(('seq', 'batch')), may hold values from 1.2159347e-11 to 4.863739e-11
- expand_second: float32 [2, 1024, 4096], P(None, ('seq', 'batch')), may hold values from 1.2159347e-10 to 4.863739e-10
- reduce_second: float32 [4096, 1024], P(('seq', 'batch')), may hold values from 1.2159348e-09 to 4.863739e-09
- gains_second: float32 [2, 1024], replicated, may hold values from 1.07288365e-08 to 4.3511392e-08
- bias_second: float32 [2, 16], replicated, may hold values from 1.2159347e-07 to 4.863739e-07
Outputs:
- layer_output: float32 [4, 1024, 1024], P('batch', 'seq')
- loss: float32 [], replicated
- input_gradient: float32 [4, 1024, 1024], P('batch', 'seq')
- grad_norm: float32 [], replicated
- attend_new: float32 [3, 1024, 1024], P(None, ('seq', 'batch'))
- attend_copy: bfloat16 [3, 1024, 1024], P(None, ('seq', 'batch'))
- attend_first_new: float32 [3, 1024, 1024], P(None, ('seq', 'batch'))
- attend_second_new: float32 [3, 1024, 1024], P(None, ('seq', 'batch'))
- output_new: float32 [1024, 1024], P(('seq', 'batch'))
- output_copy: bfloat16 [1024, 1024], P(('seq', 'batch'))
- output_first_new: float32 [1024, 1024], P(('seq', 'batch'))
- output_second_new: float32 [1024, 1024], P(('seq', 'batch'))
- expand_new: float32 [2, 1024, 4096], P(None, ('seq', 'batch'))
- expand_copy: bfloat16 [2, 1024, 4096], P(None, ('seq', 'batch'))
- expand_first_new: float32 [2, 1024, 4096], P(None, ('seq', 'batch'))
- expand_second_new: float32 [2, 1024, 4096], P(None, ('seq', 'batch'))
- reduce_new: float32 [4096, 1024], P(('seq', 'batch'))
- reduce_copy: bfloat16 [4096, 1024], P(('seq', 'batch'))
- reduce_first_new: float32 [4096, 1024], P(('seq', 'batch'))
- reduce_second_new: float32 [4096, 1024], P(('seq', 'batch'))
- gains_new: float32 [2, 1024], replicated
- gains_first_new: float32 [2, 1024], replicated
- gains_second_new: float32 [2, 1024], replicated
- bias_new: float32 [2, 16], replicated
- bias_first_new: float32 [2, 16], replicated
- bias_second_new: float32 [2, 16], replicated
Inputs may be any that keep to these rules, and one draw needn't show every extreme that they name: `variate_ids`: non-decreasing along each sequence; each of the 16 variates has one or more positions. `time_ids`: the position counted from the first position of its variate. `observed`: the first position of each sequence is 1.
All inputs are finite; a program needn't handle non-finite values.
Results may differ from a plain program's by a relative error of at most 0.012.
The roundings to bfloat16 on the way count: a program that leaves them out, or rounds other values in their place, can miss the bound.
Values may be sent and summed in bfloat16 or wider, within the bound.
A program may use at most 384 MiB of HBM per device.

v0:
```python
import functools
import math
import types

import jax
import jax.numpy as jnp
from jax import lax
from jax.experimental import pallas as pl
from jax.experimental.pallas import tpu as pltpu
from jax.sharding import PartitionSpec as P

D = 1024
HEADS = 16
HEAD_DIM = 64
STEP = 10


NORM_EPS = 1e-05
ROPE_BASE = 10000.0
MASKED = -1e30
CLIP_NORM = 1.0
BETA_ONE = 0.9
BETA_TWO = 0.98
ADAM_EPS = 1e-08
WEIGHT_DECAY = 0.1
RATE_ATTEND = 0.03
RATE_OUTPUT = 0.5
RATE_EXPAND = 0.03
RATE_REDUCE = 0.015
RATE_GAINS = 1.0
RATE_BIAS = 0.5


def angles(times):
    half_dim = HEAD_DIM // 2
    frequency = jnp.exp(-math.log(ROPE_BASE) * jnp.arange(half_dim).astype(jnp.float32) / half_dim)
    angle_table = times.astype(jnp.float32)[..., None] * frequency
    return (jnp.cos(angle_table)[..., None, :], jnp.sin(angle_table)[..., None, :])


def rotate(values, cos_table, sin_table):
    half_dim = values.shape[-1] // 2
    first_half = values[..., :half_dim]
    second_half = values[..., half_dim:]
    return jnp.concatenate(
        [
            first_half * cos_table - second_half * sin_table,
            second_half * cos_table + first_half * sin_table,
        ],
        axis=-1,
    )


def unrotate(values, cos_table, sin_table):
    half_dim = values.shape[-1] // 2
    first_half = values[..., :half_dim]
    second_half = values[..., half_dim:]
    return jnp.concatenate(
        [
            first_half * cos_table + second_half * sin_table,
            second_half * cos_table - first_half * sin_table,
        ],
        axis=-1,
    )


def normalize(values):
    inv_scale = lax.rsqrt(jnp.mean(values * values, axis=-1, keepdims=True) + NORM_EPS)
    return (values * inv_scale, inv_scale)


def norm_back(grad_act, unit_rows, inv_scale, gain_row):
    grad_unit = grad_act * gain_row
    return inv_scale * (
        grad_unit - unit_rows * jnp.mean(grad_unit * unit_rows, axis=-1, keepdims=True)
    )


def score_block(query_rows, query_labels, key_rows, key_labels, bias_table):
    scores = jnp.einsum(
        "ihe,jhe->hij", query_rows, key_rows, preferred_element_type=jnp.float32
    ) * HEAD_DIM ** (-0.5)
    same_var = query_labels[:, None] == key_labels[None, :]
    scores = scores + jnp.where(
        same_var[None], bias_table[0][:, None, None], bias_table[1][:, None, None]
    )
    scores = jnp.where(key_labels[None, None, :] >= 0, scores, MASKED)
    return (scores, same_var)


def block_grads(
    query_rows,
    query_labels,
    grad_rows,
    lse_rows,
    delta_rows,
    key_rows,
    value_rows,
    key_labels,
    bias_table,
    need_query,
    need_keys,
):
    scores, same_var = score_block(query_rows, query_labels, key_rows, key_labels, bias_table)
    weights = jnp.exp(scores - lse_rows.T[:, :, None])
    grad_weights = jnp.einsum(
        "ihe,jhe->hij", grad_rows, value_rows, preferred_element_type=jnp.float32
    )
    grad_scores = (weights * (grad_weights - delta_rows.T[:, :, None])).astype(jnp.bfloat16)
    result = ()
    if need_query:
        grad_query = jnp.einsum(
            "hij,jhe->ihe", grad_scores, key_rows, preferred_element_type=jnp.float32
        ) * HEAD_DIM ** (-0.5)
        widened = grad_scores.astype(jnp.float32)
        bias_same = jnp.sum(jnp.where(same_var[None], widened, 0.0), axis=(1, 2))
        bias_other = jnp.sum(jnp.where(same_var[None], 0.0, widened), axis=(1, 2))
        result = result + (grad_query, jnp.stack([bias_same, bias_other]))
    if need_keys:
        grad_key = jnp.einsum(
            "hij,ihe->jhe", grad_scores, query_rows, preferred_element_type=jnp.float32
        ) * HEAD_DIM ** (-0.5)
        grad_value = jnp.einsum(
            "hij,ihe->jhe",
            weights.astype(jnp.bfloat16),
            grad_rows,
            preferred_element_type=jnp.float32,
        )
        result = result + (grad_key, grad_value)
    return result


def adam_step(weight, first_moment, second_moment, gradient, step_rate, decay_rate):
    first_moment = BETA_ONE * first_moment + (1.0 - BETA_ONE) * gradient
    second_moment = BETA_TWO * second_moment + (1.0 - BETA_TWO) * gradient * gradient
    direction = (
        first_moment
        / (1.0 - BETA_ONE**STEP)
        / (jnp.sqrt(second_moment / (1.0 - BETA_TWO**STEP)) + ADAM_EPS)
    )
    return (weight - step_rate * (direction + decay_rate * weight), first_moment, second_moment)


def general_body(
    inputs,
    teacher,
    lengths,
    variate_ids,
    time_ids,
    observed,
    attend_weight,
    output_weight,
    expand_weight,
    reduce_weight,
    norm_gains,
    variate_bias,
    attend_first,
    output_first,
    expand_first,
    reduce_first,
    gains_first,
    bias_first,
    attend_second,
    output_second,
    expand_second,
    reduce_second,
    gains_second,
    bias_second,
):
    row_count = inputs.shape[1]
    length = row_count * lax.axis_size("seq")
    block_rows = math.gcd(length, 1024)
    blocks = length // block_rows
    states = inputs[0].astype(jnp.float32)
    positions = lax.axis_index("seq") * row_count + jnp.arange(row_count, dtype=jnp.int32)
    inside = positions < lengths[0]
    scored = jnp.logical_and(inside, observed[0] == 1)
    local_count = jnp.sum(scored.astype(jnp.int32))
    count_early = lax.psum(local_count, ("seq", "batch"))
    full_attend, full_output, full_expand, full_reduce = (
        lax.all_gather(attend_weight.astype(jnp.bfloat16), ("seq", "batch"), axis=1, tiled=True),
        lax.all_gather(output_weight.astype(jnp.bfloat16), ("seq", "batch"), axis=0, tiled=True),
        lax.all_gather(expand_weight.astype(jnp.bfloat16), ("seq", "batch"), axis=1, tiled=True),
        lax.all_gather(reduce_weight.astype(jnp.bfloat16), ("seq", "batch"), axis=0, tiled=True),
    )
    unit_one, scale_one = normalize(states)
    act_one = (unit_one * norm_gains[0]).astype(jnp.bfloat16)
    project = jnp.einsum("td,cde->cte", act_one, full_attend, preferred_element_type=jnp.float32)
    cos_table, sin_table = angles(time_ids[0])
    query = rotate(project[0].reshape(row_count, HEADS, HEAD_DIM), cos_table, sin_table).astype(
        jnp.bfloat16
    )
    key_rows = (
        rotate(project[1].reshape(row_count, HEADS, HEAD_DIM), cos_table, sin_table)
        .astype(jnp.bfloat16)
        .reshape(row_count, D)
    )
    value_rows = project[2].astype(jnp.bfloat16)
    own_labels = jnp.where(inside, variate_ids[0], -1).astype(jnp.bfloat16)
    all_keys, all_values, all_labels = (
        lax.all_gather(key_rows, "seq", axis=0, tiled=True),
        lax.all_gather(value_rows, "seq", axis=0, tiled=True),
        lax.all_gather(own_labels, "seq", axis=0, tiled=True),
    )
    key_blocks = all_keys.reshape(blocks, block_rows, HEADS, HEAD_DIM)
    value_blocks = all_values.reshape(blocks, block_rows, HEADS, HEAD_DIM)
    label_blocks = all_labels.astype(jnp.float32).reshape(blocks, block_rows)
    query_labels = variate_ids[0].astype(jnp.float32)

    def sweep_top(carry, pieces):
        running, sum_exp = carry
        scores, same_var = score_block(query, query_labels, pieces[0], pieces[1], variate_bias)
        raised = jnp.maximum(running, jnp.floor(jnp.max(scores, axis=-1)))
        sum_exp = sum_exp * jnp.exp(running - raised) + jnp.sum(
            jnp.exp(scores - raised[..., None]), axis=-1
        )
        return ((raised, sum_exp), None)

    start_top = jnp.full((HEADS, row_count), MASKED, jnp.float32)
    (row_top, sum_exp), unused = lax.scan(
        sweep_top,
        (start_top, jnp.zeros((HEADS, row_count), jnp.float32)),
        (key_blocks, label_blocks),
    )
    log_total = row_top + jnp.log(sum_exp)

    def sweep_out(carry, pieces):
        coarse, finest = carry
        scores, same_var = score_block(query, query_labels, pieces[0], pieces[2], variate_bias)
        weights = jnp.exp(scores - log_total[..., None])
        rounded = weights.astype(jnp.bfloat16)
        residue = (weights - rounded.astype(jnp.float32)).astype(jnp.bfloat16)
        coarse = coarse + jnp.einsum(
            "hij,jhe->ihe", rounded, pieces[1], preferred_element_type=jnp.float32
        )
        finest = finest + jnp.einsum(
            "hij,jhe->ihe", residue, pieces[1], preferred_element_type=jnp.float32
        )
        return ((coarse, finest), None)

    zero_heads = jnp.zeros((row_count, HEADS, HEAD_DIM), jnp.float32)
    (coarse, finest), unused = lax.scan(
        sweep_out, (zero_heads, zero_heads), (key_blocks, value_blocks, label_blocks)
    )
    exact_heads = coarse + finest
    mixed = coarse.reshape(row_count, D).astype(jnp.bfloat16)
    middle = states + jnp.dot(mixed, full_output, preferred_element_type=jnp.float32)
    unit_two, scale_two = normalize(middle)
    act_two = (unit_two * norm_gains[1]).astype(jnp.bfloat16)
    gate_up = jnp.einsum("td,cdf->ctf", act_two, full_expand, preferred_element_type=jnp.float32)
    sigmoid = jax.nn.sigmoid(gate_up[0])
    hidden = (gate_up[0] * sigmoid * gate_up[1]).astype(jnp.bfloat16)
    output = middle + jnp.dot(hidden, full_reduce, preferred_element_type=jnp.float32)
    error = output - teacher[0].astype(jnp.float32)
    local_square = jnp.sum(jnp.where(scored[:, None], error * error, 0.0))
    square_total = lax.psum(local_square, ("seq", "batch"))
    count_all = count_early.astype(jnp.float32)
    loss = square_total / (count_all * D)
    grad_out = jnp.where(scored[:, None], error * (2.0 / (count_all * D)), 0.0)
    back_attend, back_output, back_expand, back_reduce = (
        lax.all_gather(attend_weight.astype(jnp.bfloat16), ("seq", "batch"), axis=1, tiled=True),
        lax.all_gather(output_weight.astype(jnp.bfloat16), ("seq", "batch"), axis=0, tiled=True),
        lax.all_gather(expand_weight.astype(jnp.bfloat16), ("seq", "batch"), axis=1, tiled=True),
        lax.all_gather(reduce_weight.astype(jnp.bfloat16), ("seq", "batch"), axis=0, tiled=True),
    )
    grad_branch = grad_out.astype(jnp.bfloat16)
    reduce_grad = jnp.einsum("tf,td->fd", hidden, grad_branch, preferred_element_type=jnp.float32)
    grad_hidden = jnp.einsum(
        "td,fd->tf", grad_branch, back_reduce, preferred_element_type=jnp.float32
    )
    grad_gate = grad_hidden * gate_up[1] * sigmoid * (1.0 + gate_up[0] * (1.0 - sigmoid))
    grad_up = grad_hidden * gate_up[0] * sigmoid
    grad_expand = jnp.stack([grad_gate, grad_up]).astype(jnp.bfloat16)
    expand_grad = jnp.einsum(
        "td,ctf->cdf", act_two, grad_expand, preferred_element_type=jnp.float32
    )
    grad_act_two = jnp.einsum(
        "ctf,cdf->td", grad_expand, back_expand, preferred_element_type=jnp.float32
    )
    expand_share, reduce_share = (
        lax.psum_scatter(expand_grad, ("seq", "batch"), scatter_dimension=1, tiled=True),
        lax.psum_scatter(reduce_grad, ("seq", "batch"), scatter_dimension=0, tiled=True),
    )
    grad_middle = grad_out + norm_back(grad_act_two, unit_two, scale_two, norm_gains[1])
    grad_attn = grad_middle.astype(jnp.bfloat16)
    output_grad = jnp.einsum("td,te->de", mixed, grad_attn, preferred_element_type=jnp.float32)
    grad_mixed = jnp.einsum(
        "te,de->td", grad_attn, back_output, preferred_element_type=jnp.float32
    ).astype(jnp.bfloat16)
    grad_heads = grad_mixed.reshape(row_count, HEADS, HEAD_DIM)
    row_delta = jnp.sum(grad_heads.astype(jnp.float32) * exact_heads, axis=-1)
    lse_rows = log_total.T
    zero_bias = jnp.zeros((2, HEADS), jnp.float32)

    def sweep_query(carry, pieces):
        part_query, part_bias = block_grads(
            query,
            query_labels,
            grad_heads,
            lse_rows,
            row_delta,
            pieces[0],
            pieces[1],
            pieces[2],
            variate_bias,
            True,
            False,
        )
        return ((carry[0] + part_query, carry[1] + part_bias), None)

    (query_total, bias_grad), unused = lax.scan(
        sweep_query, (zero_heads, zero_bias), (key_blocks, value_blocks, label_blocks)
    )
    all_query, all_grad = (
        lax.all_gather(query.reshape(row_count, D), "seq", axis=0, tiled=True),
        lax.all_gather(grad_mixed, "seq", axis=0, tiled=True),
    )
    all_lse, all_delta = (
        lax.all_gather(lse_rows, "seq", axis=0, tiled=True),
        lax.all_gather(row_delta, "seq", axis=0, tiled=True),
    )
    key_heads = key_rows.reshape(row_count, HEADS, HEAD_DIM)
    value_heads = value_rows.reshape(row_count, HEADS, HEAD_DIM)
    own_float = own_labels.astype(jnp.float32)

    def sweep_keys(carry, pieces):
        part_key, part_value = block_grads(
            pieces[0],
            pieces[1],
            pieces[2],
            pieces[3],
            pieces[4],
            key_heads,
            value_heads,
            own_float,
            variate_bias,
            False,
            True,
        )
        return ((carry[0] + part_key, carry[1] + part_value), None)

    (key_total, value_heads_total), unused = lax.scan(
        sweep_keys,
        (zero_heads, zero_heads),
        (
            all_query.reshape(blocks, block_rows, HEADS, HEAD_DIM),
            label_blocks,
            all_grad.reshape(blocks, block_rows, HEADS, HEAD_DIM),
            all_lse.reshape(blocks, block_rows, HEADS),
            all_delta.reshape(blocks, block_rows, HEADS),
        ),
    )
    value_total = value_heads_total.reshape(row_count, D)
    grad_query = unrotate(query_total, cos_table, sin_table).reshape(row_count, D)
    grad_key = unrotate(key_total, cos_table, sin_table).reshape(row_count, D)
    grad_project = jnp.stack([grad_query, grad_key, value_total]).astype(jnp.bfloat16)
    attend_grad = jnp.einsum(
        "td,cte->cde", act_one, grad_project, preferred_element_type=jnp.float32
    )
    grad_act_one = jnp.einsum(
        "cte,cde->td", grad_project, back_attend, preferred_element_type=jnp.float32
    )
    attend_share, output_share = (
        lax.psum_scatter(attend_grad, ("seq", "batch"), scatter_dimension=1, tiled=True),
        lax.psum_scatter(output_grad, ("seq", "batch"), scatter_dimension=0, tiled=True),
    )
    grad_input = grad_middle + norm_back(grad_act_one, unit_one, scale_one, norm_gains[0])
    gains_grad = jnp.stack(
        [jnp.sum(grad_act_one * unit_one, axis=0), jnp.sum(grad_act_two * unit_two, axis=0)]
    )
    local_squares = (
        jnp.sum(attend_share * attend_share)
        + jnp.sum(output_share * output_share)
        + jnp.sum(expand_share * expand_share)
        + jnp.sum(reduce_share * reduce_share)
    )
    gains_total, bias_total, square_sum = lax.psum(
        (gains_grad, bias_grad, local_squares), ("seq", "batch")
    )
    grad_norm = jnp.sqrt(
        square_sum + jnp.sum(gains_total * gains_total) + jnp.sum(bias_total * bias_total)
    )
    clip_scale = jnp.minimum(1.0, CLIP_NORM / grad_norm)
    attend_new, attend_first_new, attend_second_new = adam_step(
        attend_weight,
        attend_first,
        attend_second,
        attend_share * clip_scale,
        RATE_ATTEND,
        WEIGHT_DECAY,
    )
    output_new, output_first_new, output_second_new = adam_step(
        output_weight,
        output_first,
        output_second,
        output_share * clip_scale,
        RATE_OUTPUT,
        WEIGHT_DECAY,
    )
    expand_new, expand_first_new, expand_second_new = adam_step(
        expand_weight,
        expand_first,
        expand_second,
        expand_share * clip_scale,
        RATE_EXPAND,
        WEIGHT_DECAY,
    )
    reduce_new, reduce_first_new, reduce_second_new = adam_step(
        reduce_weight,
        reduce_first,
        reduce_second,
        reduce_share * clip_scale,
        RATE_REDUCE,
        WEIGHT_DECAY,
    )
    gains_new, gains_first_new, gains_second_new = adam_step(
        norm_gains, gains_first, gains_second, gains_total * clip_scale, RATE_GAINS, 0.0
    )
    bias_new, bias_first_new, bias_second_new = adam_step(
        variate_bias, bias_first, bias_second, bias_total * clip_scale, RATE_BIAS, 0.0
    )
    input_gradient = (grad_input * count_all * D)[None]
    return (
        output[None],
        loss,
        input_gradient,
        grad_norm,
        attend_new,
        attend_new.astype(jnp.bfloat16),
        attend_first_new,
        attend_second_new,
        output_new,
        output_new.astype(jnp.bfloat16),
        output_first_new,
        output_second_new,
        expand_new,
        expand_new.astype(jnp.bfloat16),
        expand_first_new,
        expand_second_new,
        reduce_new,
        reduce_new.astype(jnp.bfloat16),
        reduce_first_new,
        reduce_second_new,
        gains_new,
        gains_first_new,
        gains_second_new,
        bias_new,
        bias_first_new,
        bias_second_new,
    )


MESH = pl.DeviceIdType.MESH
IN_VMEM = pl.BlockSpec(memory_space=pltpu.VMEM)
IN_SMEM = pl.BlockSpec(memory_space=pltpu.SMEM)
LANES = 128
HEADS_HERE = LANES // HEAD_DIM
VARIATES = 16
MIB = 1 << 20
LOW = jnp.bfloat16
WIDE = jnp.float32
TOTAL_ROWS = 24


def fast_fits(seq, batch):
    return seq == 8 and batch == 4 and seq * LANES == D


def flip(index, mask):
    result, bit = index, 1
    while bit <= mask:
        if mask & bit:
            result = result + bit - 2 * bit * lax.rem(lax.div(index, bit), 2)
        bit *= 2
    return result


def push(source, target, send_sem, recv_sem, device):
    return pltpu.make_async_remote_copy(
        src_ref=source,
        dst_ref=target,
        send_sem=send_sem,
        recv_sem=recv_sem,
        device_id=device,
        device_id_type=MESH,
    )


def block_of(index, size):
    return pl.ds(pl.multiple_of(index * size, size), size)


def dot(left, right):
    return jnp.dot(left, right, preferred_element_type=WIDE)


def dot_turned(left, right):
    return lax.dot_general(left, right, (((1,), (1,)), ((), ())), preferred_element_type=WIDE)


def turned_dot(left, right):
    return lax.dot_general(left, right, (((0,), (0,)), ((), ())), preferred_element_type=WIDE)


class Team:
    def __init__(self, index, place):
        self.index, self.place = index, place

    def at(self, mask):
        return flip(self.index, mask)


def head_team(me, group):
    return Team(me, lambda mask: (flip(me, mask), group))


def feed_team(me, group):
    return Team(
        4 * lax.rem(group, 2) + lax.rem(me, 4),
        lambda mask: (flip(me, mask % 4), flip(group, mask // 4)),
    )


class Gather:
    def __init__(self, team, rows, all_rows, sends, recvs):
        self.team, self.all_rows, self.sends, self.recvs = team, all_rows, sends, recvs
        self.size = all_rows.shape[0] // 8
        self.given = rows
        self.rows = all_rows.at[block_of(team.index, self.size)] if rows is None else rows

    def copy(self, mask, passing):
        source = self.all_rows.at[block_of(self.team.at(mask - 1 if passing else 0), self.size)]
        return push(
            source if passing else self.rows,
            source,
            self.sends.at[mask],
            self.recvs.at[mask],
            self.team.place(1 if passing else mask),
        )

    def start(self, masks=(6, 2, 4, 1)):
        for mask in masks:
            self.copy(mask, False).start()
        if self.given is not None:
            self.all_rows[block_of(self.team.index, self.size)] = self.given[...]

    def pass_on(self, chip):
        self.copy(2 * chip, False).wait_recv()
        self.copy(2 * chip + 1, True).start()

    def complete(self, chip):
        self.copy(2 * chip + 1, chip > 0).wait_recv()

    def finish(self):
        for mask in (6, 2, 4, 1):
            self.copy(mask, False).wait_send()
        for mask in (3, 5, 7):
            self.copy(mask, True).wait_send()


def at_step(step, number, *works):
    @pl.when(step == number)
    def _():
        for work in works:
            work()


def each_chip(gather, work, after):
    def one_chip(chip, unused):
        @pl.when(chip == 0)
        def _():
            gather.complete(0)

        @pl.when(chip == 1)
        def _():
            gather.pass_on(1)
            gather.pass_on(2)
            gather.copy(6, False).start()
            gather.complete(1)

        @pl.when(chip == 2)
        def _():
            gather.complete(2)

        @pl.when(chip == 3)
        def _():
            gather.pass_on(3)
            gather.complete(3)

        work(chip)
        for number, works in after.items():
            at_step(chip, number, *works)
        return unused

    lax.fori_loop(0, 4, one_chip, 0)
    gather.finish()


class Scatter:
    def __init__(self, team, buffers, near_sends, near_recvs, far_sends, far_recvs):
        self.whole, self.keep, self.near_from, self.near, self.far_from, self.far = buffers
        self.sems = near_sends, near_recvs, far_sends, far_recvs
        self.team = team
        self.size = self.keep.shape[1]

    def near_copy(self, chip):
        return push(
            self.near_from.at[chip],
            self.near.at[chip],
            self.sems[0].at[chip],
            self.sems[1].at[chip],
            self.team.place(1),
        )

    def far_copy(self, chip):
        return push(
            self.far_from.at[chip],
            self.far.at[chip],
            self.sems[2].at[chip],
            self.sems[3].at[chip],
            self.team.place(2 * chip),
        )

    def put(self, chip, rows):
        core = lax.rem(self.team.index, 2)
        self.whole[...] = rows
        self.near_from[chip] = self.whole[block_of(1 - core, self.size)].astype(LOW)
        self.near_copy(chip).start()
        self.keep[chip] = self.whole[block_of(core, self.size)]

    def combine(self, chip):
        self.near_copy(chip).wait_recv()
        self.far_from[chip] = (self.keep[chip] + self.near[chip].astype(WIDE)).astype(LOW)
        self.far_copy(chip).start()

    def total(self):
        self.near_copy(0).wait_recv()
        total = self.keep[0] + self.near[0].astype(WIDE)
        for chip in (1, 2, 3):
            self.far_copy(chip).wait_recv()
            total = total + self.far[chip].astype(WIDE)
        for chip in (0, 1, 2, 3):
            self.near_copy(chip).wait_send()
            if chip:
                self.far_copy(chip).wait_send()
        return total


class LineGather:
    def __init__(self, part_of, sends, recvs, me, group):
        self.part_of, self.sends, self.recvs, self.me, self.group = part_of, sends, recvs, me, group
        self.middle = jnp.logical_and(group >= 1, group <= 2)

    def copy(self, part, target, slot):
        return push(
            self.part_of(part),
            self.part_of(part),
            self.sends.at[slot],
            self.recvs.at[part],
            (self.me, target),
        )

    def start(self):
        group = self.group

        @pl.when(self.middle)
        def _():
            self.copy(group, 3 - group, 3 - group).start()
            self.copy(group, 3 * (group - 1), 3 * (group - 1)).start()

        @pl.when(jnp.logical_not(self.middle))
        def _():
            for step in (2, 1, 3):
                other = lax.rem(group + step, 4)
                self.copy(group, other, other).start()

    def pass_on(self):
        group = self.group

        @pl.when(self.middle)
        def _():
            self.copy(3 - group, 3 * (group - 1), group).wait_recv()
            self.copy(3 - group, 3 * (group - 1), group).start()

    def land(self):
        group = self.group

        @pl.when(self.middle)
        def _():
            for part in (0, 3):
                self.copy(part, 3 - group, group).wait_recv()

        @pl.when(jnp.logical_not(self.middle))
        def _():
            for step in (1, 2, 3):
                other = lax.rem(group + step, 4)
                self.copy(other, other, other).wait_recv()

    def finish(self):
        group = self.group

        @pl.when(self.middle)
        def _():
            for other in (3 - group, 3 * (group - 1), group):
                self.copy(group, 3 - group, other).wait_send()

        @pl.when(jnp.logical_not(self.middle))
        def _():
            for step in (1, 2, 3):
                other = lax.rem(group + step, 4)
                self.copy(group, other, other).wait_send()


class LineScatter:
    def __init__(self, part_of, landing, sends, recvs, me, group):
        self.part_of, self.landing, self.sends, self.recvs = part_of, landing, sends, recvs
        self.me, self.group = me, group
        self.middle = jnp.logical_and(group >= 1, group <= 2)
        self.opposite = 3 - 3 * lax.div(group, 2)

    def copy(self, part, slot, target, sem):
        return push(
            self.part_of(part),
            self.landing.at[slot],
            self.sends.at[sem],
            self.recvs.at[slot],
            (self.me, target),
        )

    def start(self):
        group = self.group

        @pl.when(self.middle)
        def _():
            for other in (3 - group, 3 * (group - 1)):
                self.copy(other, group, other, other).start()

        @pl.when(jnp.logical_not(self.middle))
        def _():
            beside = 1 + lax.div(group, 3)
            self.copy(3 - group, beside, beside, 3 - group).start()
            for other in (3 - beside, beside):
                self.copy(other, group, other, other).start()

    def pass_on(self):
        group, opposite = self.group, self.opposite

        @pl.when(self.middle)
        def _():
            self.copy(opposite, group, opposite, group).wait_recv()
            part = self.part_of(opposite)
            part[...] = (part[...].astype(WIDE) + self.landing[group].astype(WIDE)).astype(LOW)
            self.copy(opposite, group, opposite, group).start()

    def land(self):
        group = self.group

        @pl.when(self.middle)
        def _():
            for slot in (0, 3 - group, 3):
                self.copy(group, slot, 3 - group, group).wait_recv()

        @pl.when(jnp.logical_not(self.middle))
        def _():
            for slot in (1, 2):
                self.copy(group, slot, slot, group).wait_recv()

    def add(self, own, landed, store):
        group = self.group

        @pl.when(self.middle)
        def _():
            store(own() + landed(0) + landed(3 - group) + landed(3))

        @pl.when(jnp.logical_not(self.middle))
        def _():
            store(own() + landed(1) + landed(2))

    def finish(self):
        group = self.group

        @pl.when(self.middle)
        def _():
            for sem in (3 - group, 3 * (group - 1), group):
                self.copy(group, group, 3 - group, sem).wait_send()

        @pl.when(jnp.logical_not(self.middle))
        def _():
            for sem in (3 - group, 1, 2):
                self.copy(group, group, 1, sem).wait_send()


class QuadGather:
    def __init__(self, part_of, sends, recvs, me, group):
        self.part_of, self.sends, self.recvs = part_of, sends, recvs
        self.part = 2 * lax.div(me, 4) + lax.div(group, 2)
        self.along_y, self.along_z = (flip(me, 4), group), (me, flip(group, 2))

    def copy(self, way):
        part = self.part_of(flip(self.part, 1) if way == 3 else self.part)
        device = self.along_z if way == 1 else self.along_y
        return push(part, part, self.sends.at[way], self.recvs.at[way], device)

    def start_y(self):
        self.copy(2).start()

    def start_z(self):
        self.copy(1).start()

    def pass_on(self):
        self.copy(1).wait_recv()
        self.copy(3).start()

    def land(self):
        self.copy(2).wait_recv()
        self.copy(3).wait_recv()

    def finish(self):
        for way in (1, 2, 3):
            self.copy(way).wait_send()


class QuadScatter:
    def __init__(self, part_of, landing, sends, recvs, me, group):
        self.part_of, self.landing, self.sends, self.recvs = part_of, landing, sends, recvs
        self.part = 2 * lax.div(me, 4) + lax.div(group, 2)
        self.along_y, self.along_z = (flip(me, 4), group), (me, flip(group, 2))

    def copy(self, slot):
        return push(
            self.part_of(flip(self.part, (2, 3, 1)[slot])),
            self.landing.at[slot],
            self.sends.at[slot],
            self.recvs.at[slot],
            self.along_z if slot == 2 else self.along_y,
        )

    def start_far(self):
        self.copy(1).start()

    def start_near(self):
        self.copy(0).start()

    def pass_on(self):
        self.copy(1).wait_recv()
        part = self.part_of(flip(self.part, 1))
        part[...] = (part[...].astype(WIDE) + self.landing[1].astype(WIDE)).astype(LOW)
        self.copy(2).start()

    def land(self):
        self.copy(0).wait_recv()
        self.copy(2).wait_recv()

    def finish(self):
        for slot in (0, 1, 2):
            self.copy(slot).wait_send()


def chip_of(team, chip):
    here = lax.div(team.index, 2)
    if isinstance(chip, int):
        return flip(here, chip)
    column = lax.rem(lax.rem(here, 2) + lax.rem(chip, 2), 2)
    row = lax.rem(lax.div(here, 2) + lax.div(chip, 2), 2)
    return 2 * row + column


def turn_rows(values, cosine, sine):
    half = HEAD_DIM // 2
    pieces = []
    for start in range(0, values.shape[0], HEAD_DIM):
        first, second = values[start : start + half], values[start + half : start + HEAD_DIM]
        pieces += [first * cosine - second * sine, second * cosine + first * sine]
    return jnp.concatenate(pieces, axis=0)


def thirds(values):
    first = values.astype(LOW).astype(WIDE)
    second = (values - first).astype(LOW).astype(WIDE)
    return first, second, values - first - second


def pick(row, choices):
    result = jnp.zeros(row.shape, WIDE)
    for number, choice in choices.items():
        result = jnp.where(row == number, choice, result)
    return result


def norm_rows(values):
    scale = lax.rsqrt(jnp.mean(values * values, axis=-1, keepdims=True) + NORM_EPS)
    return values * scale, scale


def feed_block(block):
    y, x, core, far_z, near_z = (block // 16, block // 8 % 2, block // 4 % 2, block // 2 % 2, block % 2)
    return 4 * near_z + 2 * x + core, 2 * y + far_z


def layer_kernel(seq, batch, ins, outs, mem):
    me, group = lax.axis_index("seq"), lax.axis_index("batch")
    rows = ins.inputs.shape[0]
    length = rows * seq
    pair = 2 * rows
    share = ins.attend.shape[1]
    wide_columns = ins.expand.shape[2] // D
    hidden_width = mem.reduce_all.shape[0] * mem.reduce_all.shape[1]
    blocks = ins.expand.shape[2] // LANES
    heads, feeds = head_team(me, group), feed_team(me, group)
    quad = 2 * lax.div(me, 4) + lax.div(group, 2)

    staged = [(ins.attend.at[which], mem.keep.at[0, block_of(which, share)]) for which in range(3)]
    staged.append((ins.output, mem.keep.at[0, block_of(3, share)]))
    staged.append((ins.reduce, mem.keep.at[1]))
    for which in range(2):
        for block in range(wide_columns):
            columns = slice(block * D, (block + 1) * D)
            staged.append(
                (ins.expand.at[which, :, columns], mem.keep.at[2 + which, block_of(block, share)])
            )
    staged = [
        pltpu.make_async_copy(source, target, mem.stage_sem.at[number])
        for number, (source, target) in enumerate(staged)
    ]
    for copy in staged:
        copy.start()
    barrier = pltpu.get_barrier_semaphore()
    for mask in range(1, seq):
        pl.semaphore_signal(barrier, inc=1, device_id=(flip(me, mask), group), device_id_type=MESH)
    for step in range(1, batch):
        pl.semaphore_signal(
            barrier, inc=1, device_id=(me, lax.rem(group + step, batch)), device_id_type=MESH
        )
    for mask in (5, 6, 7):
        pl.semaphore_signal(barrier, inc=1, device_id=feeds.place(mask), device_id_type=MESH)

    position = me * rows + lax.broadcasted_iota(jnp.int32, (1, rows), 1)
    inside = position < ins.lengths[0]
    scored = jnp.logical_and(inside, ins.observed[...] == 1).astype(WIDE)
    variate = ins.variates[...].astype(WIDE)
    turns = ins.turns.shape[0]
    mem.facts_own[:turns] = ins.turns[...]
    mem.facts_own[turns:] = jnp.concatenate(
        [jnp.where(inside, variate, -1.0), variate, scored, jnp.zeros((5, rows), WIDE)], axis=0
    )
    mem.scored[...] = jnp.broadcast_to(scored, (rows, rows)).T
    unit_one, scale_one = norm_rows(ins.inputs[...].astype(WIDE))
    mem.own_rows[0] = (unit_one * ins.gains[0:1, :]).astype(LOW)
    for copy in staged:
        copy.wait()
    for which in range(3):
        mem.attend_low[which] = mem.keep[0, block_of(which, share)].astype(LOW)
    mem.output_full[block_of(batch * me + group, share)] = mem.keep[0, block_of(3, share)].astype(LOW)
    mem.reduce_all[quad] = mem.keep[1].astype(LOW)
    for which in range(2):
        for block in range(blocks):
            owner, part = feed_block(block)
            row, lane = divmod(block * LANES, D)
            mem.expand_low[which, owner, :, part * LANES : (part + 1) * LANES] = mem.keep[
                2 + which, block_of(row, share), lane : lane + LANES
            ].astype(LOW)
    pl.semaphore_wait(barrier, seq + batch + 1)

    masks = (6, 7, 4, 5, 2, 3, 1)

    def start_attend_columns():
        copies = []
        for mask in masks:
            copy = push(
                mem.attend_low.at[:, :, block_of(heads.at(mask), LANES)],
                mem.attend_all.at[:, me, group],
                mem.column_send.at[0, mask],
                mem.column_recv.at[0, mask],
                heads.place(mask),
            )
            copy.start()
            copies.append(copy)
        mem.attend_all[:, me, group] = mem.attend_low[:, :, block_of(me, LANES)]
        return copies

    def start_expand_columns():
        copies = []
        for mask in masks:
            copy = push(
                mem.expand_low.at[:, feeds.at(mask)],
                mem.expand_all.at[:, me, group],
                mem.column_send.at[1, mask],
                mem.column_recv.at[1, mask],
                feeds.place(mask),
            )
            copy.start()
            copies.append(copy)
        mem.expand_all[:, me, group] = mem.expand_low[:, feeds.index]
        return copies

    def expand_part_of(array, which):
        def part_of(part):
            return array.at[which, pl.ds(4 * lax.div(part, 2), 4), pl.ds(2 * lax.rem(part, 2), 2)]

        return part_of

    def line_gather(row, part_of):
        return LineGather(part_of, mem.line_send.at[row], mem.line_recv.at[row], me, group)

    def quad_gather(row, part_of):
        return QuadGather(part_of, mem.line_send.at[row], mem.line_recv.at[row], me, group)

    def gather(team, phase, all_rows):
        return Gather(
            team,
            mem.own_rows.at[phase],
            all_rows,
            mem.gather_send.at[phase],
            mem.gather_recv.at[phase],
        )

    def scatter(team, phase):
        return Scatter(
            team,
            (mem.whole, mem.keep, mem.near_from, mem.near, mem.far_from, mem.far),
            mem.near_send.at[phase],
            mem.near_recv.at[phase],
            mem.far_send.at[phase],
            mem.far_recv.at[phase],
        )

    attend_columns = start_attend_columns()
    line_output = line_gather(1, lambda part: mem.output_full.at[block_of(batch * me + part, share)])
    line_output.start()
    facts = Gather(heads, mem.facts_own, mem.facts_all, mem.facts_send, mem.facts_recv)
    facts.start()
    for copy in attend_columns:
        copy.wait_recv()
    line_attend = line_gather(0, lambda part: mem.attend_all.at[:, :, part])
    line_attend.start()
    acts = gather(heads, 0, mem.act_one)
    acts.start()
    for chip in (1, 2, 3):
        facts.pass_on(chip)
    for chip in (0, 1, 2, 3):
        facts.complete(chip)
    facts.finish()
    step_rows = mem.facts_own.shape[0]
    half = HEAD_DIM // 2
    count = jnp.zeros((8, LANES), WIDE)
    for slot in range(seq):
        columns = slice(slot * rows, (slot + 1) * rows)
        start = slot * step_rows
        mem.cosine[:, columns] = mem.facts_all[start : start + half]
        mem.sine[:, columns] = mem.facts_all[start + half : start + 2 * half]
        labels = mem.facts_all[start + 2 * half : start + 2 * half + 8]
        mem.labels[:, columns] = labels
        count = count + labels
    mem.count[group] = count
    count_copies = []
    for step in range(1, batch):
        copy = push(
            mem.count.at[group],
            mem.count.at[group],
            mem.count_send.at[step],
            mem.count_recv.at[step],
            (me, lax.rem(group + step, batch)),
        )
        copy.start()
        count_copies.append(copy)

    def mark(block, unused):
        span = block_of(block, pair)
        row = lax.broadcasted_iota(jnp.int32, (HEAD_DIM, pair), 0)
        third = lax.div(row, VARIATES)
        variate = lax.rem(row, VARIATES).astype(WIDE)
        key_label, query_label = mem.labels[0:1, span], mem.labels[1:2, span]
        ones = jnp.ones((1, pair), WIDE)
        last = 3 * VARIATES
        hidden_keys = (key_label < 0.0).astype(WIDE)
        mem.key_marks[:, span] = jnp.where(
            third < 3,
            (key_label == variate).astype(WIDE),
            pick(row, {last: ones, last + 1: ones, last + 2: ones, last + 3: hidden_keys}),
        ).astype(LOW)
        query_marks = (query_label == variate).astype(WIDE)
        mem.sum_marks[:, span] = jnp.where(
            row < VARIATES, query_marks, pick(row, {VARIATES: ones})
        ).astype(LOW)
        for head in range(HEADS_HERE):
            number = me * HEADS_HERE + head
            other = jnp.full((HEAD_DIM, pair), ins.bias[1, number], WIDE)
            more = thirds(jnp.full((HEAD_DIM, pair), ins.bias[0, number], WIDE) - other)
            other = thirds(other)
            mem.query_turned[head, HEAD_DIM:, span] = jnp.where(
                third < 3,
                query_marks * jnp.where(third == 0, more[0], jnp.where(third == 1, more[1], more[2])),
                pick(row, {last: other[0], last + 1: other[1], last + 2: other[2], last + 3: MASKED}),
            ).astype(LOW)
        return unused

    lax.fori_loop(0, length // pair, mark, 0)
    acts.pass_on(1)
    acts.pass_on(2)
    line_output.pass_on()
    line_output.land()
    outputs = Gather(heads, None, mem.output_full, mem.output_send, mem.output_recv)
    outputs.start()
    acts.pass_on(3)
    line_attend.pass_on()
    for chip in range(4):
        acts.complete(chip)
    acts.finish()

    expand_columns = start_expand_columns()
    line_reduce = quad_gather(4, lambda part: mem.reduce_all.at[part])
    line_reduce.start_z()
    line_expand = [
        quad_gather(2 + which, expand_part_of(mem.expand_all, which)) for which in range(2)
    ]
    line_attend.land()
    line_reduce.start_y()

    def attend_matrix(which):
        return mem.attend_all[which].reshape(D, LANES)

    def project(block, unused):
        span = block_of(block, pair)
        act = mem.act_one[span, :]
        cosine, sine = mem.cosine[:, span], mem.sine[:, span]
        query = turn_rows(dot(act, attend_matrix(0)).T, cosine, sine).astype(LOW)
        query = (query.astype(WIDE) * HEAD_DIM ** (-0.5)).astype(LOW)
        key = turn_rows(dot(act, attend_matrix(1)).T, cosine, sine).astype(LOW)
        value = dot(act, attend_matrix(2)).T.astype(LOW)
        mem.key_turned[:, span] = key
        mem.value_turned[:, span] = value

        for head in range(HEADS_HERE):
            features = slice(head * HEAD_DIM, (head + 1) * HEAD_DIM)
            mem.query_turned[head, :HEAD_DIM, span] = query[features]
            whole = jnp.concatenate([key[features], mem.key_marks[:, span]], axis=0)
            mem.key_heads[head, span, :] = whole.T
        return unused

    for copy in expand_columns:
        copy.wait_recv()
    line_expand[0].start_z()
    line_expand[0].start_y()
    lax.fori_loop(0, length // pair, project, 0)
    line_expand[1].start_z()
    outputs.pass_on(1)
    outputs.pass_on(2)

    core = lax.rem(me, 2)

    def mixed_copy(chip, which):
        other = 2 * chip_of(heads, chip) + which
        slot = 2 * chip + lax.rem(which + core, 2)
        return push(
            mem.mixed_out.at[block_of(other, rows)],
            mem.mixed_rows.at[:, block_of(me, LANES)],
            mem.mixed_send.at[slot],
            mem.mixed_recv.at[slot],
            (other, group),
        )

    def attend_block(chip):
        columns = block_of(chip_of(heads, chip), pair)
        for head in range(HEADS_HERE):
            span = slice(head * HEAD_DIM, (head + 1) * HEAD_DIM)
            scores = dot(mem.key_heads[head], mem.query_turned[head, :, columns])
            top = jnp.floor(jnp.max(scores, axis=0, keepdims=True))
            powers = jnp.exp(scores - top)
            probs = powers * (1.0 / jnp.sum(powers, axis=0, keepdims=True))
            rounded = probs.astype(LOW)
            mem.probs[head, :, columns] = rounded
            residue = (probs - rounded.astype(WIDE)).astype(LOW)
            coarse = dot(mem.value_turned[span, :], rounded)
            mem.exact[span, columns] = coarse + dot(mem.value_turned[span, :], residue)
            mem.mixed_wide[span, :] = coarse
        mixed = mem.mixed_wide[...].astype(LOW)
        mem.mixed_turned[:, columns] = mixed
        mem.mixed_out[columns, :] = mixed.T

    def attend_step(step, unused):
        chip = lax.rem(step + 1, 4)
        attend_block(chip)
        for which in range(2):

            @pl.when(jnp.logical_or(chip > 0, core != which))
            def _():
                mixed_copy(chip, which).start()

        at_step(step, 1, lambda: outputs.pass_on(3))
        return unused

    lax.fori_loop(0, 4, attend_step, 0)
    line_expand[1].start_y()
    mem.mixed_rows[:, block_of(me, LANES)] = mem.mixed_out[block_of(me, rows), :]
    for chip in range(4):
        outputs.complete(chip)
    outputs.finish()

    def wait_pieces(copy):
        for mask in range(1, seq):
            copy(mask).wait()

    def mixed_wait(mask):
        other = heads.at(mask)
        return push(
            mem.mixed_out.at[block_of(other, rows)],
            mem.mixed_rows.at[:, block_of(other, LANES)],
            mem.mixed_send.at[mask],
            mem.mixed_recv.at[mask],
            (other, group),
        )

    wait_pieces(mixed_wait)
    middle = ins.inputs[...].astype(WIDE) + dot(mem.mixed_rows[...], mem.output_full[...])
    mem.middle[...] = middle
    unit_two, scale_two = norm_rows(middle)
    mem.own_rows[1] = (unit_two * ins.gains[1:2, :]).astype(LOW)
    acts = gather(feeds, 1, mem.act_two)
    acts.start((2, 4, 1))
    line_reduce.pass_on()
    line_expand[0].pass_on()

    def split_heads(block, unused):
        span = block_of(block, pair)
        row = lax.broadcasted_iota(jnp.int32, (HEAD_DIM, pair), 0)
        value_marks = jnp.where(row < 3, 1.0, 0.0).astype(LOW)
        for head in range(HEADS_HERE):
            features = slice(head * HEAD_DIM, (head + 1) * HEAD_DIM)
            value = mem.value_turned[features, span]
            mem.value_heads[head, span, :] = jnp.concatenate([value, value_marks], axis=0).T
            query = mem.query_turned[head, :HEAD_DIM, span]
            whole = jnp.concatenate([query, mem.sum_marks[:, span]], axis=0)
            mem.query_heads[head, span, :] = whole.T
        return unused

    lax.fori_loop(0, length // pair, split_heads, 0)
    line_expand[0].land()

    def expand_matrix(which):
        return mem.expand_all[which].reshape(D, hidden_width)

    def reduce_matrix():
        return mem.reduce_all[...].reshape(hidden_width, D)

    def feed_gate(chip):
        span = block_of(chip_of(feeds, chip), pair)
        mem.by_gate[span, :] = dot(mem.act_two[span, :], expand_matrix(0))

    def feed_up(chip, unused=0):
        span = block_of(chip_of(feeds, chip), pair)
        gate = mem.by_gate[span, :]
        up = dot(mem.act_two[span, :], expand_matrix(1))
        sigmoid = 1.0 / (1.0 + jnp.exp(-gate))
        swish = gate * sigmoid
        mem.by_up[span, :] = swish
        mem.by_gate[span, :] = up * sigmoid * (1.0 + gate * (1.0 - sigmoid))
        mem.hidden[span, :] = (swish * up).astype(LOW)
        return unused

    each_chip(
        acts,
        feed_gate,
        {
            0: [line_expand[1].pass_on],
            2: [line_expand[1].land, lambda: lax.fori_loop(0, 3, feed_up, 0)],
            3: [lambda: lax.fori_loop(3, 4, feed_up, 0)],
        },
    )
    line_reduce.land()
    sums = scatter(feeds, 1)

    def feed_down(step, unused):
        chip = lax.rem(step + 1, 4)
        span = block_of(chip_of(feeds, chip), pair)
        sums.put(chip, dot(mem.hidden[span, :], reduce_matrix()))
        at_step(step, 1, lambda: sums.combine(1))
        at_step(step, 2, lambda: sums.combine(2))
        return unused

    lax.fori_loop(0, 4, feed_down, 0)
    sums.combine(3)

    for block in range(length // pair):
        span = block_of(block, pair)
        mem.hidden_turned[:, span] = mem.hidden[span, :].T
        mem.act_two_turned[:, span] = mem.act_two[span, :].T
    output = mem.middle[...] + sums.total()
    outs.layer_output[...] = output
    for copy in count_copies:
        copy.wait()
    count_all = jnp.sum(
        mem.count[0, 2:3] + mem.count[1, 2:3] + mem.count[2, 2:3] + mem.count[3, 2:3],
        axis=1,
        keepdims=True,
    )
    error = jnp.where(mem.scored[:, 0:1] > 0.0, output - ins.teacher[...].astype(WIDE), 0.0)
    mem.squares[1:2, :] = jnp.sum(error * error, axis=0, keepdims=True)
    grad_out = error * (2.0 / (count_all * D))
    mem.grad_own[...] = grad_out
    mem.own_rows[2] = grad_out.astype(LOW)
    acts = gather(feeds, 2, mem.branch)
    acts.start((2, 4, 1))

    sums = scatter(feeds, 2)

    def feed_back(chip):
        span = block_of(chip_of(feeds, chip), pair)
        grad_hidden = dot_turned(mem.branch[span, :], reduce_matrix())
        grad_gate = (grad_hidden * mem.by_gate[span, :]).astype(LOW)
        grad_up = (grad_hidden * mem.by_up[span, :]).astype(LOW)
        mem.grad_gate[span, :] = grad_gate
        mem.grad_up[span, :] = grad_up
        sums.put(
            chip,
            dot_turned(grad_gate, expand_matrix(0)) + dot_turned(grad_up, expand_matrix(1)),
        )

    each_chip(acts, feed_back, {2: [lambda: sums.combine(1)], 3: [lambda: sums.combine(2)]})

    def line_scatter(row, part_of, landing):
        return LineScatter(
            part_of, landing, mem.back_send.at[row], mem.back_recv.at[row], me, group
        )

    def quad_scatter(row, part_of, landing):
        return QuadScatter(
            part_of, landing, mem.back_send.at[row], mem.back_recv.at[row], me, group
        )

    def reduce_grad(part, unused):
        mem.reduce_grad[part] = dot(
            mem.hidden_turned[block_of(part, rows), :], mem.branch[...]
        ).astype(LOW)
        at_step(part, 0, lambda: sums.combine(3))
        return unused

    lax.fori_loop(0, batch, reduce_grad, 0)
    back_reduce = quad_scatter(0, lambda part: mem.reduce_grad.at[part], mem.reduce_land)
    back_reduce.start_far()

    def expand_grad(which):
        grads = (mem.grad_gate, mem.grad_up)[which]

        def one_block(block, unused):
            products = dot(mem.act_two_turned[block_of(block, pair), :], grads[...]).astype(LOW)
            mem.expand_grad[which, pl.ds(2 * block, 2)] = products.reshape(
                2, batch, share, hidden_width
            )
            return unused

        lax.fori_loop(0, seq // 2, one_block, 0)
        line = quad_scatter(
            1 + which, expand_part_of(mem.expand_grad, which), mem.expand_land.at[which]
        )
        return line

    back_expand = []
    back_expand.append(expand_grad(0))
    back_expand[0].start_far()
    grad_act = sums.total()
    unit_two, scale_two = norm_rows(mem.middle[...])
    gain = ins.gains[1:2, :]
    grad_unit = grad_act * gain
    mem.gains[1:2, :] = jnp.sum(grad_act * unit_two, axis=0, keepdims=True)
    grad_middle = mem.grad_own[...] + scale_two * (
        grad_unit - unit_two * jnp.mean(grad_unit * unit_two, axis=-1, keepdims=True)
    )
    mem.grad_own[...] = grad_middle
    mem.own_rows[3] = grad_middle.astype(LOW)
    grad_mixed = dot(mem.output_full[...], grad_middle.T.astype(LOW)).astype(LOW)
    mem.grad_mixed_out[...] = grad_mixed.reshape(seq, LANES, rows)

    def grad_copy(mask, back=False):
        return push(
            mem.grad_mixed_out.at[heads.at(mask)],
            mem.grad_mixed.at[:, block_of(heads.at(mask) if back else me, rows)],
            mem.mixed_send.at[8 + mask],
            mem.mixed_recv.at[8 + mask],
            heads.place(mask),
        )

    for mask in masks:
        grad_copy(mask).start()
    mem.grad_mixed[:, block_of(me, rows)] = mem.grad_mixed_out[me]
    back_reduce.pass_on()
    back_expand.append(expand_grad(1))
    back_expand[1].start_far()

    wait_pieces(lambda mask: grad_copy(mask, True))
    acts = gather(heads, 3, mem.grad_attn)
    acts.start()
    back_reduce.start_near()
    back_expand[0].start_near()
    back_attend = [
        line_scatter(
            4 + which,
            lambda part, which=which: mem.attend_grad.at[which, :, part],
            mem.attend_land.at[which],
        )
        for which in range(3)
    ]

    def attend_grad(which):
        grads = dot(mem.grad_project[which], mem.act_one[...])
        mem.attend_grad[which] = grads.T.astype(LOW).reshape(seq, batch, share, LANES)
        back_attend[which].start()

    lane = lax.broadcasted_iota(jnp.int32, (pair, LANES), 1)

    def grad_rows(block, unused):
        span = block_of(block, pair)
        whole = mem.grad_mixed[:, span].astype(WIDE).T
        for head in range(HEADS_HERE):
            mem.grad_heads[head, span, :] = jnp.where(lax.div(lane, HEAD_DIM) == head, whole, 0.0).astype(LOW)
        return unused

    lax.fori_loop(0, length // pair, grad_rows, 0)

    def value_back(block, unused):
        span = block_of(block, pair)
        total = dot(mem.probs[0, span, :], mem.grad_heads[0])
        for head in range(1, HEADS_HERE):
            total = total + dot(mem.probs[head, span, :], mem.grad_heads[head])
        mem.grad_project[2, :, span] = total.T.astype(LOW)
        return unused

    lax.fori_loop(0, length // pair, value_back, 0)
    back_expand[0].pass_on()
    attend_grad(2)

    def score_back(block, unused):
        columns = block_of(block, pair)
        row = lax.broadcasted_iota(jnp.int32, (HEAD_DIM, pair), 0)
        grads = mem.grad_mixed[:, columns]
        delta = grads.astype(WIDE) * mem.exact[:, columns]
        for head in range(HEADS_HERE):
            span = slice(head * HEAD_DIM, (head + 1) * HEAD_DIM)
            pieces = thirds(-jnp.sum(delta[span], axis=0, keepdims=True))
            marks = pick(row, dict(enumerate(pieces))).astype(LOW)
            change = dot(mem.value_heads[head], jnp.concatenate([grads[span], marks], axis=0))
            mem.probs[head, :, columns] = (mem.probs[head, :, columns].astype(WIDE) * change).astype(LOW)
        return unused

    lax.fori_loop(0, length // pair, score_back, 0)
    back_expand[1].start_near()
    mem.bias_sums[...] = jnp.zeros_like(mem.bias_sums)
    scale = HEAD_DIM ** (-0.5)

    def project_grads(block, unused):
        span = block_of(block, pair)
        cosine, sine = mem.cosine[:, span], -mem.sine[:, span]
        queries, keys = [], []
        for head in range(HEADS_HERE):
            features = slice(head * HEAD_DIM, (head + 1) * HEAD_DIM)
            queries.append(dot(mem.key_turned[features, :], mem.probs[head, :, span]) * scale)
            sums = dot(mem.probs[head, span, :], mem.query_heads[head]).T
            keys.append(sums[:HEAD_DIM])
            by_variate = sums[HEAD_DIM : HEAD_DIM + VARIATES]
            same = by_variate * mem.key_marks[:VARIATES, span].astype(WIDE)
            mem.bias_sums[head : head + 1, :] += jnp.sum(same, axis=0, keepdims=True)
            total = sums[HEAD_DIM + VARIATES : HEAD_DIM + VARIATES + 1]
            mem.bias_sums[HEADS_HERE + head : HEADS_HERE + head + 1, :] += total
        mem.grad_project[0, :, span] = turn_rows(jnp.concatenate(queries, axis=0), cosine, sine).astype(LOW)
        mem.grad_project[1, :, span] = turn_rows(jnp.concatenate(keys, axis=0), cosine, sine).astype(LOW)
        return unused

    lax.fori_loop(0, length // pair, project_grads, 0)
    back_expand[1].pass_on()
    attend_grad(0)
    acts.pass_on(1)
    acts.pass_on(2)
    sums = scatter(heads, 3)

    def project_back(step, unused):
        chip = lax.rem(step + 1, 4)
        span = block_of(chip_of(heads, chip), pair)
        total = jnp.zeros((pair, D), WIDE)
        for which in range(3):
            total = total + dot_turned(mem.grad_project[which, :, span].T, attend_matrix(which))
        sums.put(chip, total)
        at_step(step, 1, lambda: sums.combine(1))
        at_step(step, 2, lambda: sums.combine(2))
        return unused

    lax.fori_loop(0, 4, project_back, 0)
    sums.combine(3)
    attend_grad(1)
    acts.pass_on(3)
    for chip in range(4):
        acts.complete(chip)
    acts.finish()
    mem.output_grad[...] = (
        dot(mem.mixed_turned[...], mem.grad_attn[...]).astype(LOW).reshape(mem.output_grad.shape)
    )
    back_output = line_scatter(3, lambda part: mem.output_grad.at[part], mem.output_land)
    back_output.start()
    for which in (2, 0, 1):
        back_attend[which].pass_on()

    column_copies = []
    mem.squares[0:1, :] = jnp.zeros((1, D), WIDE)

    def add_squares(total):
        flat = total.reshape(-1, total.shape[-1])
        width = flat.shape[1]
        mem.squares[0:1, :width] += jnp.sum(flat * flat, axis=0, keepdims=True)

    def store_whole(total, out):
        out[...] = total
        add_squares(total)

    back_reduce.land()
    store_whole(
        mem.reduce_grad[quad].astype(WIDE)
        + mem.reduce_land[0].astype(WIDE)
        + mem.reduce_land[2].astype(WIDE),
        outs.reduce_share,
    )
    def expand_shares(which):
        back_expand[which].land()
        own = expand_part_of(mem.expand_grad, which)(quad)

        def one_block(block, unused):
            total = (
                own[block].astype(WIDE)
                + mem.expand_land[which, 0, block].astype(WIDE)
                + mem.expand_land[which, 2, block].astype(WIDE)
            )
            mem.expand_part[which, block] = total.astype(LOW)
            add_squares(total)
            return unused

        lax.fori_loop(0, 4, one_block, 0)
        for mask in masks:
            other = feeds.at(mask)
            copy = push(
                mem.expand_part.at[which, lax.rem(other, 4), lax.div(other, 4)],
                mem.expand_share.at[which, feeds.index],
                mem.share_send.at[which, mask],
                mem.share_recv.at[which, mask],
                feeds.place(mask),
            )
            copy.start()
            column_copies.append(copy)
        mem.expand_share[which, feeds.index] = mem.expand_part[
            which, lax.rem(feeds.index, 4), lax.div(feeds.index, 4)
        ]

    for which in range(2):
        expand_shares(which)

    def attend_shares(which):
        back_attend[which].land()

        def store(total):
            mem.attend_part[which] = total.astype(LOW)
            add_squares(total)

        back_attend[which].add(
            lambda: mem.attend_grad[which, :, group].astype(WIDE),
            lambda slot: mem.attend_land[which, slot].astype(WIDE),
            store,
        )

    attend_shares(2)
    grad_act = sums.total()
    unit_one, scale_one = norm_rows(ins.inputs[...].astype(WIDE))
    gain = ins.gains[0:1, :]
    grad_unit = grad_act * gain
    mem.gains[0:1, :] = jnp.sum(grad_act * unit_one, axis=0, keepdims=True)
    grad_input = mem.grad_own[...] + scale_one * (
        grad_unit - unit_one * jnp.mean(grad_unit * unit_one, axis=-1, keepdims=True)
    )
    outs.input_gradient[...] = grad_input * (count_all * D)
    outs.count[...] = jnp.broadcast_to(count_all, (8, LANES))

    back_output.pass_on()
    for which in range(2):
        attend_shares(which)
    for mask in masks:
        copy = push(
            mem.attend_part.at[:, heads.at(mask)],
            outs.attend_share.at[:, :, block_of(me, LANES)],
            mem.share_send.at[2, mask],
            mem.share_recv.at[2, mask],
            heads.place(mask),
        )
        copy.start()
        column_copies.append(copy)
    outs.attend_share[:, :, block_of(me, LANES)] = mem.attend_part[:, me]
    back_output.land()
    back_output.add(
        lambda: mem.output_grad[group].astype(WIDE),
        lambda slot: mem.output_land[slot].astype(WIDE),
        lambda total: store_whole(total, outs.output_share),
    )

    lane = lax.broadcasted_iota(jnp.int32, (1, LANES), 1)
    lines = [
        mem.gains[which : which + 1, start : start + LANES]
        for which in range(2)
        for start in range(0, D, LANES)
    ]
    bias_line = jnp.zeros((1, LANES), WIDE)
    for row in range(2 * HEADS_HERE):
        place = row // HEADS_HERE * HEADS + me * HEADS_HERE + row % HEADS_HERE
        line = mem.bias_sums[row : row + 1, :]
        if row >= HEADS_HERE:
            line = line - mem.bias_sums[row - HEADS_HERE : row - HEADS_HERE + 1, :]
        amount = jnp.sum(line, axis=1, keepdims=True)
        bias_line = bias_line + jnp.where(lane == place, amount, 0.0)
    amounts = jnp.sum(mem.squares[0:2, :], axis=1, keepdims=True)
    amount_line = jnp.where(lane == 0, amounts[0:1], 0.0) + jnp.where(lane == 1, amounts[1:2], 0.0)
    lines += [bias_line, amount_line, jnp.zeros((6, LANES), WIDE)]
    mem.plane_totals[me] = jnp.concatenate(lines, axis=0)
    plane_copies = []
    for mask in masks:
        copy = push(
            mem.plane_totals.at[me],
            mem.plane_totals.at[me],
            mem.total_send.at[0, mask],
            mem.total_recv.at[0, mask],
            (flip(me, mask), group),
        )
        copy.start()
        plane_copies.append(copy)
    for copy in column_copies[: 2 * len(masks)]:
        copy.wait()
    for which in range(2):
        for block in range(blocks):
            owner, part = feed_block(block)
            outs.expand_share[which, :, block * LANES : (block + 1) * LANES] = mem.expand_share[
                which, owner, :, part * LANES : (part + 1) * LANES
            ]
    for copy in plane_copies:
        copy.wait()
    mem.line_totals[group] = jnp.sum(mem.plane_totals[...], axis=0)
    total_copies = []
    for step in range(1, batch):
        copy = push(
            mem.line_totals.at[group],
            mem.line_totals.at[group],
            mem.total_send.at[1, step],
            mem.total_recv.at[1, step],
            (me, lax.rem(group + step, batch)),
        )
        copy.start()
        total_copies.append(copy)
    for copy in total_copies:
        copy.wait()
    outs.totals[...] = jnp.sum(mem.line_totals[...], axis=0)
    for copy in column_copies[2 * len(masks) :]:
        copy.wait()
    for copies in (attend_columns, expand_columns):
        for copy in copies:
            copy.wait_send()
    for line in [line_attend, line_output, line_reduce] + line_expand:
        line.finish()
    for line in [back_output, back_reduce] + back_attend + back_expand:
        line.finish()


def call_layer(seq, batch, inputs, teacher, lengths, variates, observed, turns, bias, gains, attend, output, expand, reduce):
    rows, share, hidden = inputs.shape[0], attend.shape[1], expand.shape[2] // seq
    length, pair, chips = rows * seq, 2 * rows, seq // 2
    low = lambda *shape: pltpu.VMEM(shape, LOW)
    wide = lambda *shape: pltpu.VMEM(shape, WIDE)
    sems = lambda *shape: pltpu.SemaphoreType.DMA(shape)
    in_names = ["inputs", "teacher", "lengths", "variates", "observed", "turns", "bias", "gains"]
    in_names += ["attend", "output", "expand", "reduce"]
    outs = dict(
        layer_output=((rows, D), WIDE),
        input_gradient=((rows, D), WIDE),
        totals=((TOTAL_ROWS, LANES), WIDE),
        count=((8, LANES), WIDE),
        attend_share=((3, share, D), LOW),
        output_share=((output.shape[0], D), WIDE),
        expand_share=((2, share, hidden * seq), LOW),
        reduce_share=((reduce.shape[0], D), WIDE),
    )
    scratch = dict(
        gains=wide(2, D),
        squares=wide(8, D),
        plane_totals=wide(seq, TOTAL_ROWS, LANES),
        line_totals=wide(batch, TOTAL_ROWS, LANES),
        attend_low=low(3, share, D),
        expand_low=low(2, seq, share, hidden),
        attend_all=low(3, seq, batch, share, LANES),
        output_full=low(D, D),
        expand_all=low(2, seq, batch, share, hidden),
        reduce_all=low(batch, reduce.shape[0], D),
        own_rows=low(4, rows, D),
        act_one=low(length, D),
        act_two=low(length, D),
        branch=low(length, D),
        grad_attn=low(length, D),
        facts_own=wide(turns.shape[0] + 8, LANES),
        facts_all=wide(seq * (turns.shape[0] + 8), LANES),
        scored=wide(rows, LANES),
        cosine=wide(HEAD_DIM // 2, length),
        sine=wide(HEAD_DIM // 2, length),
        labels=wide(8, length),
        key_marks=low(HEAD_DIM, length),
        count=wide(batch, 8, LANES),
        query_turned=low(HEADS_HERE, LANES, length),
        key_turned=low(LANES, length),
        value_turned=low(LANES, length),
        key_heads=low(HEADS_HERE, length, LANES),
        value_heads=low(HEADS_HERE, length, LANES),
        query_heads=low(HEADS_HERE, length, LANES),
        grad_heads=low(HEADS_HERE, length, LANES),
        grad_mixed=low(LANES, length),
        grad_mixed_out=low(seq, LANES, rows),
        probs=low(HEADS_HERE, length, length),
        mixed_out=low(length, LANES),
        mixed_rows=low(rows, D),
        sum_marks=low(HEAD_DIM, length),
        hidden_turned=low(hidden, length),
        act_two_turned=low(D, length),
        exact=wide(LANES, length),
        mixed_wide=wide(LANES, pair),
        mixed_turned=low(LANES, length),
        whole=wide(pair, D),
        keep=wide(chips, rows, D),
        near_from=low(chips, rows, D),
        near=low(chips, rows, D),
        far_from=low(chips, rows, D),
        far=low(chips, rows, D),
        middle=wide(rows, D),
        grad_own=wide(rows, D),
        by_up=wide(length, hidden),
        by_gate=wide(length, hidden),
        hidden=low(length, hidden),
        grad_gate=low(length, hidden),
        grad_up=low(length, hidden),
        bias_sums=wide(8, pair),
        grad_project=low(3, LANES, length),
        reduce_grad=low(batch, reduce.shape[0], D),
        expand_grad=low(2, seq, batch, share, hidden),
        output_grad=low(batch, output.shape[0], D),
        attend_grad=low(3, seq, batch, share, LANES),
        reduce_land=low(3, reduce.shape[0], D),
        expand_land=low(2, 3, 4, 2, share, hidden),
        output_land=low(batch, output.shape[0], D),
        attend_land=low(3, batch, seq, share, LANES),
        expand_part=low(2, 4, 2, share, hidden),
        expand_share=low(2, seq, share, hidden),
        attend_part=low(3, seq, share, LANES),
        stage_sem=sems(5 + 2 * (expand.shape[2] // D)),
        total_send=sems(2, seq),
        total_recv=sems(2, seq),
        column_send=sems(2, seq),
        column_recv=sems(2, seq),
        line_send=sems(5, batch),
        line_recv=sems(5, batch),
        facts_send=sems(seq),
        facts_recv=sems(seq),
        gather_send=sems(4, seq),
        gather_recv=sems(4, seq),
        count_send=sems(batch),
        count_recv=sems(batch),
        near_send=sems(4, chips),
        near_recv=sems(4, chips),
        far_send=sems(4, chips),
        far_recv=sems(4, chips),
        back_send=sems(7, batch),
        back_recv=sems(7, batch),
        output_send=sems(seq),
        output_recv=sems(seq),
        mixed_send=sems(2 * seq),
        mixed_recv=sems(2 * seq),
        share_send=sems(3, seq),
        share_recv=sems(3, seq),
    )

    places = dict.fromkeys(("attend", "output", "expand", "reduce"), pl.BlockSpec(memory_space=pl.ANY))
    places["bias"] = places["lengths"] = IN_SMEM

    def kernel(*refs):
        groups, start = [], 0
        for names in (in_names, outs, scratch):
            names = list(names)
            groups.append(types.SimpleNamespace(**dict(zip(names, refs[start : start + len(names)]))))
            start += len(names)
        layer_kernel(seq, batch, *groups)

    results = pl.pallas_call(
        kernel,
        out_shape=[jax.ShapeDtypeStruct(*out) for out in outs.values()],
        in_specs=[places.get(name, IN_VMEM) for name in in_names],
        out_specs=[IN_VMEM] * len(outs),
        scratch_shapes=list(scratch.values()),
        compiler_params=pltpu.CompilerParams(
            collective_id=0, has_side_effects=True, vmem_limit_bytes=63 * MIB
        ),
        name="layer",
    )(inputs, teacher, lengths, variates, observed, turns, bias, gains, attend, output, expand, reduce)
    return types.SimpleNamespace(**dict(zip(outs, results)))


def update_kernel(
    smalls, ins, small_outs, outs, olds, shares, news, copies, passed, in_sems, out_sems
):
    totals, count, gains, gains_first, gains_second, bias, bias_first, bias_second = smalls
    order = (2, 3, 0, 1)
    comes = []
    for place, number in enumerate(order):
        pairs = list(zip(ins[4 + 3 * number : 7 + 3 * number], olds[3 * number : 3 * number + 3]))
        pairs.append((ins[number], shares[number]))
        comes.append(
            [
                pltpu.make_async_copy(source, target, in_sems.at[4 * place + part])
                for part, (source, target) in enumerate(pairs)
            ]
        )
    for copy in sum(comes, []):
        copy.start()
    through = [
        pltpu.make_async_copy(ins[16 + part], passed[part], in_sems.at[16 + part]) for part in range(2)
    ]
    for copy in through:
        copy.start()
    goes = []
    gains_total = jnp.concatenate(
        [
            jnp.concatenate([totals[row + i : row + i + 1, :] for i in range(D // LANES)], axis=1)
            for row in (0, D // LANES)
        ],
        axis=0,
    )
    row = 2 * D // LANES
    bias_total = jnp.concatenate(
        [totals[row : row + 1, :HEADS], totals[row : row + 1, HEADS : 2 * HEADS]], axis=0
    )
    row += 1

    def sum_all(values):
        return jnp.sum(jnp.sum(values, axis=0, keepdims=True), axis=1, keepdims=True)

    squares = (
        totals[row : row + 1, 0:1] + sum_all(gains_total * gains_total) + sum_all(bias_total * bias_total)
    )
    grad_norm = jnp.sqrt(squares)
    clip = jnp.minimum(1.0, CLIP_NORM / grad_norm)
    small_outs[0][...] = totals[row : row + 1, 1:2] / (count[0:1, 0:1] * D)
    small_outs[1][...] = grad_norm
    rates = (RATE_ATTEND, RATE_OUTPUT, RATE_EXPAND, RATE_REDUCE)
    for place, number in enumerate(order):
        for copy in comes[place]:
            copy.wait()
        weight, first, second = olds[3 * number : 3 * number + 3]
        new, first_new, second_new = news[3 * number : 3 * number + 3]
        arrays = (new, copies[number], first_new, second_new, weight, first, second, shares[number])
        for lead in range(weight.shape[0] if weight.ndim == 3 else 1):

            def one_block(block, unused, lead=lead, arrays=arrays, rate=rates[number]):
                rows = block_of(block, 16)
                place = (lead, rows) if arrays[0].ndim == 3 else (rows,)
                old, moment, square, share = [array[place] for array in arrays[4:]]
                step = fast_step(old, moment, square, share.astype(WIDE) * clip, rate)
                arrays[0][place], arrays[2][place], arrays[3][place] = step
                arrays[1][place] = step[0].astype(LOW)
                return unused

            lax.fori_loop(0, weight.shape[-2] // 16, one_block, 0)
        for part, source in enumerate((new, copies[number], first_new, second_new)):
            copy = pltpu.make_async_copy(
                source, outs[2 + 4 * number + part], out_sems.at[2 + 4 * number + part]
            )
            copy.start()
            goes.append(copy)
        if place == 0:
            for part in range(2):
                through[part].wait()
                copy = pltpu.make_async_copy(passed[part], outs[part], out_sems.at[part])
                copy.start()
                goes.append(copy)
    for number, (old, total, rate) in enumerate(
        (
            ((gains, gains_first, gains_second), gains_total, RATE_GAINS),
            ((bias, bias_first, bias_second), bias_total, RATE_BIAS),
        )
    ):
        new, first_new, second_new = small_outs[2 + 3 * number : 5 + 3 * number]
        new[...], first_new[...], second_new[...] = adam_step(
            old[0][...], old[1][...], old[2][...], total * clip, rate, 0.0
        )
    for copy in goes:
        copy.wait()


def fast_step(weight, first, second, gradient, rate):
    first = BETA_ONE * first + (1.0 - BETA_ONE) * gradient
    second = BETA_TWO * second + ((1.0 - BETA_TWO) * gradient) * gradient
    low = jnp.sqrt(second * (1.0 / (1.0 - BETA_TWO**STEP))) + ADAM_EPS
    step = first * (rate / (1.0 - BETA_ONE**STEP)) / low
    return weight * (1.0 - rate * WEIGHT_DECAY) - step, first, second


def call_update(done, shares, smalls, olds):
    in_hbm = pl.BlockSpec(memory_space=pl.ANY)
    smalls = [done.totals, done.count] + smalls
    ins = shares + olds + [done.layer_output, done.input_gradient]
    one = jax.ShapeDtypeStruct((1, 1), WIDE)
    small_outs = [one, one] + smalls[2:]
    outs = [(done.layer_output, WIDE), (done.input_gradient, WIDE)]
    for weight in olds[::3]:
        outs += [(weight, dtype) for dtype in (WIDE, LOW, WIDE, WIDE)]
    passed = ins[-2:]
    parts = [smalls, ins, small_outs, outs, olds, shares, olds, olds[::3], passed]

    def kernel(*refs):
        groups, start = [], 0
        for part in parts:
            groups.append(refs[start : start + len(part)])
            start += len(part)
        update_kernel(*groups, *refs[start:])

    results = pl.pallas_call(
        kernel,
        out_shape=[jax.ShapeDtypeStruct(array.shape, WIDE) for array in small_outs]
        + [jax.ShapeDtypeStruct(array.shape, dtype) for array, dtype in outs],
        in_specs=[IN_VMEM] * len(smalls) + [in_hbm] * len(ins),
        out_specs=[IN_VMEM] * len(small_outs) + [in_hbm] * len(outs),
        scratch_shapes=[pltpu.VMEM(array.shape, WIDE) for array in olds]
        + [pltpu.VMEM(array.shape, array.dtype) for array in shares]
        + [pltpu.VMEM(array.shape, WIDE) for array in olds]
        + [pltpu.VMEM(array.shape, LOW) for array in olds[::3]]
        + [pltpu.VMEM(array.shape, WIDE) for array in passed]
        + [pltpu.SemaphoreType.DMA((18,)), pltpu.SemaphoreType.DMA((18,))],
        compiler_params=pltpu.CompilerParams(vmem_limit_bytes=63 * MIB),
        name="update",
    )(*smalls, *ins)
    return results[: len(small_outs)], results[len(small_outs) :]


def fast_body(
    seq,
    batch,
    inputs,
    teacher,
    lengths,
    variate_ids,
    time_ids,
    observed,
    attend_weight,
    output_weight,
    expand_weight,
    reduce_weight,
    norm_gains,
    variate_bias,
    attend_first,
    output_first,
    expand_first,
    reduce_first,
    gains_first,
    bias_first,
    attend_second,
    output_second,
    expand_second,
    reduce_second,
    gains_second,
    bias_second,
):
    half_dim = HEAD_DIM // 2
    frequency = jnp.exp(-math.log(ROPE_BASE) * jnp.arange(half_dim).astype(WIDE) / half_dim)
    angle = frequency[:, None] * time_ids.astype(WIDE)
    done = call_layer(
        seq,
        batch,
        inputs[0],
        teacher[0],
        lengths,
        variate_ids,
        observed,
        jnp.concatenate([jnp.cos(angle), jnp.sin(angle)]),
        variate_bias,
        norm_gains,
        attend_weight,
        output_weight,
        expand_weight,
        reduce_weight,
    )
    small, large = call_update(
        done,
        [done.attend_share, done.output_share, done.expand_share, done.reduce_share],
        [norm_gains, gains_first, gains_second, variate_bias, bias_first, bias_second],
        [attend_weight, attend_first, attend_second]
        + [output_weight, output_first, output_second]
        + [expand_weight, expand_first, expand_second]
        + [reduce_weight, reduce_first, reduce_second],
    )
    return (
        large[0][None],
        small[0].reshape(()),
        large[1][None],
        small[1].reshape(()),
    ) + tuple(large[2:] + small[2:])


def solution(mesh):
    seq, batch = mesh.shape["seq"], mesh.shape["batch"]
    body = functools.partial(fast_body, seq, batch) if fast_fits(seq, batch) else general_body
    in_specs = (
        P("batch", "seq", None),
        P("batch", "seq", None),
        P("batch"),
        P("batch", "seq"),
        P("batch", "seq"),
        P("batch", "seq"),
        P(None, ("seq", "batch"), None),
        P(("seq", "batch"), None),
        P(None, ("seq", "batch"), None),
        P(("seq", "batch"), None),
        P(),
        P(),
        P(None, ("seq", "batch"), None),
        P(("seq", "batch"), None),
        P(None, ("seq", "batch"), None),
        P(("seq", "batch"), None),
        P(),
        P(),
        P(None, ("seq", "batch"), None),
        P(("seq", "batch"), None),
        P(None, ("seq", "batch"), None),
        P(("seq", "batch"), None),
        P(),
        P(),
    )
    out_specs = (
        P("batch", "seq", None),
        P(),
        P("batch", "seq", None),
        P(),
        P(None, ("seq", "batch"), None),
        P(None, ("seq", "batch"), None),
        P(None, ("seq", "batch"), None),
        P(None, ("seq", "batch"), None),
        P(("seq", "batch"), None),
        P(("seq", "batch"), None),
        P(("seq", "batch"), None),
        P(("seq", "batch"), None),
        P(None, ("seq", "batch"), None),
        P(None, ("seq", "batch"), None),
        P(None, ("seq", "batch"), None),
        P(None, ("seq", "batch"), None),
        P(("seq", "batch"), None),
        P(("seq", "batch"), None),
        P(("seq", "batch"), None),
        P(("seq", "batch"), None),
        P(),
        P(),
        P(),
        P(),
        P(),
        P(),
    )
    return jax.shard_map(body, mesh=mesh, in_specs=in_specs, out_specs=out_specs, check_vma=False)
```

profile of v0, /device:TPU:0, one launch (start us, length us, event | category | flops | bytes accessed | tf_op | source)
XLA Modules:
  0.0 209.1 jit_solution(9796241017836711432)
XLA Ops:
  1.3 0.0 copy-start
  1.3 0.6 copy-done
  2.0 0.1 multiply_cosine_fusion
  2.1 0.6 pad_maximum_fusion.refs_5_
  2.8 197.9 %layer.1 = (f32[128,1024]{1,0:T(8,128)}, f32[128,1024]{1,0:T(8,128)}, f32[24,128]{1,0:T(8,128)}, f32[8,128]{1,0:T(8,128)}, bf16[3,32,1024]{2,1,0:T(8,128)(2,1)},...) custom-call(bf16[128,1024]{1,0:T(8,128)(2,1)} %bitcast.8, bf16[128,1024]{1,0:T(8,128)(2,1)} %bitcast.9, ...), custom_call_target="tpu_custom_call" | custom-call | tf_op jit(solution)/shard_map/layer/pallas_call | solution.py:1787
  200.6 8.3 %update.1 = (f32[1,1]{1,0:T(1,128)}, f32[1,1]{1,0:T(1,128)}, f32[2,1024]{1,0:T(2,128)}, f32[2,1024]{1,0:T(2,128)}, f32[2,1024]{1,0:T(2,128)}, /*index=5*/f32[2,1...) custom-call(f32[24,128]{1,0:T(8,128)} %get-tuple-element.60.refs_0_,, ...), custom_call_target="tpu_custom_call" | custom-call | tf_op jit(solution)/shard_map/update/pallas_call | solution.py:1919
  (2 shorter events, 0.0 us)
Async XLA Ops:
  1.3 0.7 copy-start
where the time goes:
time: 209 us
  Pallas kernels  206 us (99%)
    pallas_call x1, Pallas kernels, call_layer(): pl.pallas_call(kernel, out_shape=[jax.ShapeDtypeStruct(*out) for out in o...  198 us
    pallas_call x1, Pallas kernels, call_update(): pl.pallas_call(kernel, out_shape=[jax.ShapeDtypeStruct(array.shape, WIDE)...  8.32 us

commit v1 on v0

--- a/solution.py
+++ b/solution.py
@@ -4,6 +4,7 @@
 
 import jax
 import jax.numpy as jnp
+import numpy as np
 from jax import lax
 from jax.experimental import pallas as pl
 from jax.experimental.pallas import tpu as pltpu
@@ -938,27 +939,17 @@
     inside = position < ins.lengths[0]
     scored = jnp.logical_and(inside, ins.observed[...] == 1).astype(WIDE)
     variate = ins.variates[...].astype(WIDE)
-    turns = ins.turns.shape[0]
-    mem.facts_own[:turns] = ins.turns[...]
-    mem.facts_own[turns:] = jnp.concatenate(
+    angle = ins.frequency[...] * ins.times[...].astype(WIDE)
+    mem.facts_own[: HEAD_DIM // 2] = jnp.cos(angle)
+    mem.facts_own[HEAD_DIM // 2 : HEAD_DIM] = jnp.sin(angle)
+    mem.facts_own[HEAD_DIM:] = jnp.concatenate(
         [jnp.where(inside, variate, -1.0), variate, scored, jnp.zeros((5, rows), WIDE)], axis=0
     )
     mem.scored[...] = jnp.broadcast_to(scored, (rows, rows)).T
-    unit_one, scale_one = norm_rows(ins.inputs[...].astype(WIDE))
-    mem.own_rows[0] = (unit_one * ins.gains[0:1, :]).astype(LOW)
     for copy in staged:
         copy.wait()
     for which in range(3):
         mem.attend_low[which] = mem.keep[0, block_of(which, share)].astype(LOW)
-    mem.output_full[block_of(batch * me + group, share)] = mem.keep[0, block_of(3, share)].astype(LOW)
-    mem.reduce_all[quad] = mem.keep[1].astype(LOW)
-    for which in range(2):
-        for block in range(blocks):
-            owner, part = feed_block(block)
-            row, lane = divmod(block * LANES, D)
-            mem.expand_low[which, owner, :, part * LANES : (part + 1) * LANES] = mem.keep[
-                2 + which, block_of(row, share), lane : lane + LANES
-            ].astype(LOW)
     pl.semaphore_wait(barrier, seq + batch + 1)
 
     masks = (6, 7, 4, 5, 2, 3, 1)
@@ -1025,8 +1016,19 @@
         )
 
     attend_columns = start_attend_columns()
+    mem.output_full[block_of(batch * me + group, share)] = mem.keep[0, block_of(3, share)].astype(LOW)
+    mem.reduce_all[quad] = mem.keep[1].astype(LOW)
+    for which in range(2):
+        for block in range(blocks):
+            owner, part = feed_block(block)
+            row, lane = divmod(block * LANES, D)
+            mem.expand_low[which, owner, :, part * LANES : (part + 1) * LANES] = mem.keep[
+                2 + which, block_of(row, share), lane : lane + LANES
+            ].astype(LOW)
     line_output = line_gather(1, lambda part: mem.output_full.at[block_of(batch * me + part, share)])
     line_output.start()
+    unit_one, scale_one = norm_rows(ins.inputs[...].astype(WIDE))
+    mem.own_rows[0] = (unit_one * ins.gains[0:1, :]).astype(LOW)
     facts = Gather(heads, mem.facts_own, mem.facts_all, mem.facts_send, mem.facts_recv)
     facts.start()
     for copy in attend_columns:
@@ -1660,13 +1662,14 @@
         line.finish()
 
 
-def call_layer(seq, batch, inputs, teacher, lengths, variates, observed, turns, bias, gains, attend, output, expand, reduce):
+def call_layer(seq, batch, inputs, teacher, lengths, variates, observed, times, frequency, bias, gains, attend, output, expand, reduce):
     rows, share, hidden = inputs.shape[0], attend.shape[1], expand.shape[2] // seq
     length, pair, chips = rows * seq, 2 * rows, seq // 2
     low = lambda *shape: pltpu.VMEM(shape, LOW)
     wide = lambda *shape: pltpu.VMEM(shape, WIDE)
     sems = lambda *shape: pltpu.SemaphoreType.DMA(shape)
-    in_names = ["inputs", "teacher", "lengths", "variates", "observed", "turns", "bias", "gains"]
+    in_names = ["inputs", "teacher", "lengths", "variates", "observed"]
+    in_names += ["times", "frequency", "bias", "gains"]
     in_names += ["attend", "output", "expand", "reduce"]
     outs = dict(
         layer_output=((rows, D), WIDE),
@@ -1694,8 +1697,8 @@
         act_two=low(length, D),
         branch=low(length, D),
         grad_attn=low(length, D),
-        facts_own=wide(turns.shape[0] + 8, LANES),
-        facts_all=wide(seq * (turns.shape[0] + 8), LANES),
+        facts_own=wide(HEAD_DIM + 8, LANES),
+        facts_all=wide(seq * (HEAD_DIM + 8), LANES),
         scored=wide(rows, LANES),
         cosine=wide(HEAD_DIM // 2, length),
         sine=wide(HEAD_DIM // 2, length),
@@ -1794,7 +1797,7 @@
             collective_id=0, has_side_effects=True, vmem_limit_bytes=63 * MIB
         ),
         name="layer",
-    )(inputs, teacher, lengths, variates, observed, turns, bias, gains, attend, output, expand, reduce)
+    )(inputs, teacher, lengths, variates, observed, times, frequency, bias, gains, attend, output, expand, reduce)
     return types.SimpleNamespace(**dict(zip(outs, results)))
 
 
@@ -1963,8 +1966,8 @@
     bias_second,
 ):
     half_dim = HEAD_DIM // 2
-    frequency = jnp.exp(-math.log(ROPE_BASE) * jnp.arange(half_dim).astype(WIDE) / half_dim)
-    angle = frequency[:, None] * time_ids.astype(WIDE)
+    frequency = np.exp(-math.log(ROPE_BASE) * np.arange(half_dim) / half_dim).astype(np.float32)
+    frequency = np.broadcast_to(frequency[:, None], (half_dim, LANES))
     done = call_layer(
         seq,
         batch,
@@ -1973,7 +1976,8 @@
         lengths,
         variate_ids,
         observed,
-        jnp.concatenate([jnp.cos(angle), jnp.sin(angle)]),
+        time_ids,
+        jnp.asarray(frequency),
         variate_bias,
         norm_gains,
         attend_weight,

time: 209 us -> 209 us (level)
  no operation moved by 1% of the time
where the time goes in v1:
time: 209 us
  Pallas kernels  206 us (99%)
    pallas_call x1, Pallas kernels, call_layer(): pl.pallas_call(kernel, out_shape=[jax.ShapeDtypeStruct(*out) for out in o...  198 us
    pallas_call x1, Pallas kernels, call_update(): pl.pallas_call(kernel, out_shape=[jax.ShapeDtypeStruct(array.shape, WIDE)...  8.32 us

profile of v1, /device:TPU:0, one launch (start us, length us, event | category | flops | bytes accessed | tf_op | source)
XLA Modules:
  0.0 209.2 jit_solution(9459787414657634994)
XLA Ops:
  1.3 0.0 copy-start
  1.3 0.6 copy-done
  2.0 0.7 jit_solution_.3.refs_6_
  2.6 198.1 %layer.1 = (f32[128,1024]{1,0:T(8,128)}, f32[128,1024]{1,0:T(8,128)}, f32[24,128]{1,0:T(8,128)}, f32[8,128]{1,0:T(8,128)}, bf16[3,32,1024]{2,1,0:T(8,128)(2,1)},...) custom-call(bf16[128,1024]{1,0:T(8,128)(2,1)} %bitcast.6, bf16[128,1024]{1,0:T(8,128)(2,1)} %bitcast.7, ...), custom_call_target="tpu_custom_call" | custom-call | tf_op jit(solution)/shard_map/layer/pallas_call | solution.py:1790
  200.7 8.3 %update.1 = (f32[1,1]{1,0:T(1,128)}, f32[1,1]{1,0:T(1,128)}, f32[2,1024]{1,0:T(2,128)}, f32[2,1024]{1,0:T(2,128)}, f32[2,1024]{1,0:T(2,128)}, /*index=5*/f32[2,1...) custom-call(f32[24,128]{1,0:T(8,128)} %get-tuple-element.60.refs_0_,, ...), custom_call_target="tpu_custom_call" | custom-call | tf_op jit(solution)/shard_map/update/pallas_call | solution.py:1922
Async XLA Ops:
  1.3 0.7 copy-start

commit v2 on v1

--- a/solution.py
+++ b/solution.py
@@ -936,10 +936,12 @@
         pl.semaphore_signal(barrier, inc=1, device_id=feeds.place(mask), device_id_type=MESH)
 
     position = me * rows + lax.broadcasted_iota(jnp.int32, (1, rows), 1)
-    inside = position < ins.lengths[0]
+    inside = position < ins.lengths[...]
     scored = jnp.logical_and(inside, ins.observed[...] == 1).astype(WIDE)
     variate = ins.variates[...].astype(WIDE)
-    angle = ins.frequency[...] * ins.times[...].astype(WIDE)
+    half_dim = HEAD_DIM // 2
+    number = lax.broadcasted_iota(jnp.int32, (half_dim, rows), 0).astype(WIDE)
+    angle = jnp.exp(-math.log(ROPE_BASE) * number / half_dim) * ins.times[...].astype(WIDE)
     mem.facts_own[: HEAD_DIM // 2] = jnp.cos(angle)
     mem.facts_own[HEAD_DIM // 2 : HEAD_DIM] = jnp.sin(angle)
     mem.facts_own[HEAD_DIM:] = jnp.concatenate(
@@ -1662,14 +1664,14 @@
         line.finish()
 
 
-def call_layer(seq, batch, inputs, teacher, lengths, variates, observed, times, frequency, bias, gains, attend, output, expand, reduce):
+def call_layer(seq, batch, inputs, teacher, lengths, variates, observed, times, bias, gains, attend, output, expand, reduce):
     rows, share, hidden = inputs.shape[0], attend.shape[1], expand.shape[2] // seq
     length, pair, chips = rows * seq, 2 * rows, seq // 2
     low = lambda *shape: pltpu.VMEM(shape, LOW)
     wide = lambda *shape: pltpu.VMEM(shape, WIDE)
     sems = lambda *shape: pltpu.SemaphoreType.DMA(shape)
     in_names = ["inputs", "teacher", "lengths", "variates", "observed"]
-    in_names += ["times", "frequency", "bias", "gains"]
+    in_names += ["times", "bias", "gains"]
     in_names += ["attend", "output", "expand", "reduce"]
     outs = dict(
         layer_output=((rows, D), WIDE),
@@ -1777,7 +1779,7 @@
     )
 
     places = dict.fromkeys(("attend", "output", "expand", "reduce"), pl.BlockSpec(memory_space=pl.ANY))
-    places["bias"] = places["lengths"] = IN_SMEM
+    places["bias"] = IN_SMEM
 
     def kernel(*refs):
         groups, start = [], 0
@@ -1797,7 +1799,7 @@
             collective_id=0, has_side_effects=True, vmem_limit_bytes=63 * MIB
         ),
         name="layer",
-    )(inputs, teacher, lengths, variates, observed, times, frequency, bias, gains, attend, output, expand, reduce)
+    )(inputs, teacher, lengths, variates, observed, times, bias, gains, attend, output, expand, reduce)
     return types.SimpleNamespace(**dict(zip(outs, results)))
 
 
@@ -1857,15 +1859,17 @@
         for lead in range(weight.shape[0] if weight.ndim == 3 else 1):
 
             def one_block(block, unused, lead=lead, arrays=arrays, rate=rates[number]):
-                rows = block_of(block, 16)
-                place = (lead, rows) if arrays[0].ndim == 3 else (rows,)
+                across = arrays[0].shape[-1] // D
+                rows = block_of(lax.div(block, across), 16)
+                columns = block_of(lax.rem(block, across), D)
+                place = (lead, rows, columns) if len(arrays[0].shape) == 3 else (rows, columns)
                 old, moment, square, share = [array[place] for array in arrays[4:]]
                 step = fast_step(old, moment, square, share.astype(WIDE) * clip, rate)
                 arrays[0][place], arrays[2][place], arrays[3][place] = step
                 arrays[1][place] = step[0].astype(LOW)
                 return unused
 
-            lax.fori_loop(0, weight.shape[-2] // 16, one_block, 0)
+            lax.fori_loop(0, weight.shape[-2] // 16 * (weight.shape[-1] // D), one_block, 0)
         for part, source in enumerate((new, copies[number], first_new, second_new)):
             copy = pltpu.make_async_copy(
                 source, outs[2 + 4 * number + part], out_sems.at[2 + 4 * number + part]
@@ -1965,19 +1969,15 @@
     gains_second,
     bias_second,
 ):
-    half_dim = HEAD_DIM // 2
-    frequency = np.exp(-math.log(ROPE_BASE) * np.arange(half_dim) / half_dim).astype(np.float32)
-    frequency = np.broadcast_to(frequency[:, None], (half_dim, LANES))
     done = call_layer(
         seq,
         batch,
         inputs[0],
         teacher[0],
-        lengths,
+        lengths[:, None],
         variate_ids,
         observed,
         time_ids,
-        jnp.asarray(frequency),
         variate_bias,
         norm_gains,
         attend_weight,

time: 209 us -> 208 us (level)
  no operation moved by 1% of the time
where the time goes in v2:
time: 208 us
  Pallas kernels  207 us (100%)
    pallas_call x1, Pallas kernels, call_layer(): pl.pallas_call(kernel, out_shape=[jax.ShapeDtypeStruct(*out) for out in o...  198 us
    pallas_call x1, Pallas kernels, call_update(): pl.pallas_call(kernel, out_shape=[jax.ShapeDtypeStruct(array.shape, WIDE)...  8.39 us

profile of v2, /device:TPU:0, one launch (start us, length us, event | category | flops | bytes accessed | tf_op | source)
XLA Modules:
  0.0 208.0 jit_solution(8915985366851810839)
XLA Ops:
  1.3 198.1 %layer.1 = (f32[128,1024]{1,0:T(8,128)}, f32[128,1024]{1,0:T(8,128)}, f32[24,128]{1,0:T(8,128)}, f32[8,128]{1,0:T(8,128)}, bf16[3,32,1024]{2,1,0:T(8,128)(2,1)},...) custom-call(bf16[128,1024]{1,0:T(8,128)(2,1)} %bitcast.8, bf16[128,1024]{1,0:T(8,128)(2,1)} %bitcast.9, ...), custom_call_target="tpu_custom_call" | custom-call | tf_op jit(solution)/shard_map/layer/pallas_call | solution.py:1792
  199.4 8.4 %update.1 = (f32[1,1]{1,0:T(1,128)}, f32[1,1]{1,0:T(1,128)}, f32[2,1024]{1,0:T(2,128)}, f32[2,1024]{1,0:T(2,128)}, f32[2,1024]{1,0:T(2,128)}, /*index=5*/f32[2,1...) custom-call(f32[24,128]{1,0:T(8,128)} %get-tuple-element.60.refs_0_,, ...), custom_call_target="tpu_custom_call" | custom-call | tf_op jit(solution)/shard_map/update/pallas_call | solution.py:1926
